TPU v7x, 32 devices: a whole 2x2x4 slice. The times are simulated.
32 devices in a mesh: tp: 2 (over core), ep: 16 (over z, y, x).
Axes of the slice: x: 2, y: 2, z: 4, core: 2. Of those that a mesh axis runs over, the one named last changes fastest.
Arguments:
- context: bfloat16 [16, 256, 2048], P('ep', None, 'tp'), may hold values from -6 to 6
- out_weight: bfloat16 [2048, 2048], P('tp'), may hold values from -0.125 to 0.125
- residual_in: bfloat16 [16, 256, 2048], P('ep', 'tp'), may hold values from -6 to 6
- norm_gain: float32 [2048], replicated, may hold values from 0.5 to 1.5
- expert_ids: int32 [16, 256, 2], P('ep', 'tp'), may hold values from 0 to 15, all different within a row; in each aligned block of 128 rows (0 to 127, 128 to 255, ..., all dimensions but the last counted through in order) at most 24 rows name the same one
- gate_weights: float32 [16, 256, 2], P('ep', 'tp'), may hold values from 0.2 to 1
- keep_mask: int32 [16, 256, 2], P('ep', 'tp'), may hold values 0 or 1
- expert_in: bfloat16 [16, 2048, 4096], P('ep', None, 'tp'), may hold values from -0.125 to 0.125
- expert_out: bfloat16 [16, 4096, 2048], P('ep', 'tp'), may hold values from -0.09375 to 0.09375
Outputs:
- layer_out: bfloat16 [16, 256, 2048], P('ep', 'tp')
Inputs may be any that keep to these rules, and one draw needn't show every extreme that they name: `expert_ids`: among the 128 tokens of one device (aligned blocks of token rows), at most 24 name any one expert; a token's two experts differ; every expert is named somewhere.
All inputs are finite; a program needn't handle non-finite values. No bound on the sum of `keep_mask` on one device may be relied on, other than what follows from the above.
Results may differ from a plain program's by a relative error of at most 0.0054.
Values may be sent and summed in bfloat16 or wider, within the bound.
A program may use at most 128 MiB of HBM per device.

v0:
```python
import jax
import jax.numpy as jnp
from jax import lax
from jax.sharding import PartitionSpec as P


def expert_ffn(picked_rows, weight_in, weight_out):
    hidden = jnp.maximum(
        jnp.einsum("smd,df->smf", picked_rows, weight_in, preferred_element_type=jnp.float32), 0.0
    ).astype(jnp.bfloat16)
    return jnp.einsum("smf,fd->smd", hidden, weight_out, preferred_element_type=jnp.float32)


def body(
    context,
    out_weight,
    residual_in,
    norm_gain,
    expert_ids,
    gate_weights,
    keep_mask,
    expert_in,
    expert_out,
):
    tok_rows = residual_in.shape[1]
    feature_count = residual_in.shape[2]
    local_context = context[0]
    attended = lax.psum_scatter(
        jnp.dot(local_context, out_weight, preferred_element_type=jnp.float32),
        "tp",
        scatter_dimension=0,
        tiled=True,
    )
    stream = (residual_in[0].astype(jnp.float32) + attended).astype(jnp.bfloat16)
    stream_f32 = stream.astype(jnp.float32)
    average = jnp.mean(stream_f32, axis=1, keepdims=True)
    centred = stream_f32 - average
    variance = jnp.mean(centred * centred, axis=1, keepdims=True)
    normed = (centred / jnp.sqrt(variance + 1e-05) * norm_gain[None, :]).astype(jnp.bfloat16)
    expert_count = lax.axis_size("ep")
    capacity = 3 * tok_rows // expert_count
    total_slots = expert_count * capacity
    routed = expert_ids[0].reshape(-1)
    kept_flags = keep_mask[0].reshape(-1)
    assign_count = routed.shape[0]
    onehot = (routed[:, None] == jnp.arange(expert_count, dtype=jnp.int32)[None, :]).astype(
        jnp.int32
    ) * kept_flags[:, None]
    rank_table = jnp.cumsum(onehot, axis=0) - onehot
    rank_own = jnp.sum(rank_table * onehot, axis=1)
    slot_index = jnp.where(kept_flags > 0, routed * capacity + rank_own, -1)
    slot_match = (slot_index[None, :] == jnp.arange(total_slots, dtype=jnp.int32)[:, None]).astype(
        jnp.int32
    )
    source = jnp.sum(slot_match * jnp.arange(assign_count, dtype=jnp.int32)[None, :], axis=1)
    filled = jnp.sum(slot_match, axis=1)
    outgoing = jnp.where(filled[:, None] > 0, normed[source // 2], jnp.zeros((), jnp.bfloat16))
    outgoing = outgoing.reshape(expert_count, capacity, feature_count)
    weight_in = expert_in[0]
    weight_out = expert_out[0]
    doubled = jnp.concatenate([outgoing, outgoing], axis=0)
    partial_value = expert_ffn(
        lax.all_to_all(doubled, ("tp", "ep"), split_axis=0, concat_axis=0, tiled=True),
        weight_in,
        weight_out,
    )
    halves_back = lax.all_to_all(
        partial_value, ("tp", "ep"), split_axis=0, concat_axis=0, tiled=True
    )
    returned = jnp.sum(
        halves_back.reshape(2, expert_count, capacity, feature_count), axis=0
    ).astype(jnp.bfloat16)
    returned = returned.reshape(total_slots, feature_count)
    pulled = returned[jnp.maximum(slot_index, 0)].astype(jnp.float32)
    gate_flat = jnp.where(kept_flags > 0, gate_weights[0].reshape(-1), 0.0)
    mixed = jnp.sum((gate_flat[:, None] * pulled).reshape(tok_rows, 2, feature_count), axis=1)
    layer_out = (stream_f32 + mixed).astype(jnp.bfloat16)
    return layer_out[None]


def solution(mesh):
    return jax.shard_map(
        body,
        mesh=mesh,
        in_specs=(
            P("ep", None, "tp"),
            P("tp", None),
            P("ep", "tp", None),
            P(),
            P("ep", "tp", None),
            P("ep", "tp", None),
            P("ep", "tp", None),
            P("ep", None, "tp"),
            P("ep", "tp", None),
        ),
        out_specs=P("ep", "tp", None),
        check_vma=False,
    )
```

profile of v0, /device:TPU:0, one launch (start us, length us, event | category | flops | bytes accessed | tf_op | source)
XLA Modules:
  0.0 296.4 jit_solution(5737100319545325864)
XLA Ops:
  6.5 0.0 copy-start
  6.5 0.0 copy-start.3
  6.5 0.0 copy-start.4
  6.5 0.0 copy-start.1
  6.5 0.0 reduce-scatter.2.cloned.1.call-start
  6.6 1.0 copy-done
  7.6 4.8 %fusion.16 = f32[256,2048]{1,0:T(8,128)} fusion(bf16[1024,2048]{1,0:T(8,128)(2,1)} %param.10, bf16[1,256,1024]{2,1,0:T(8,128)(2,1)S(1)} %copy-done), kind=kOutput, calls=%fused_computation.22 | convolution fusion | flops 1073741824 | bytes 6815744 | tf_op jit(solution)/shard_map/dot_general | solution.py:29
  12.4 0.0 copy-start.2
  12.4 0.0 reduce-scatter.2.cloned.1.call-update
  12.4 0.0 copy-done.3
  12.4 0.1 copy.20
  12.5 0.1 mul.72
  12.7 0.1 reshape_squeeze.7
  12.8 0.0 copy-done.4
  12.8 0.1 copy.21
  12.9 0.1 eq.36
  13.1 0.1 reshape_squeeze.8
  13.2 0.6 reduce-window.6
  13.8 0.2 slice_reduce_fusion
  14.0 0.1 fusion.18
  14.1 0.2 convert_reduce_fusion.1
  14.4 0.1 gt.44
  14.5 10.3 %reduce-scatter.2.cloned.1.call-done = f32[128,2048]{1,0:T(8,128)} async-done(((f32[256,2048]{1,0:T(8,128)}), f32[128,2048]{1,0:T(8,128)}) %reduce-scatter.2.cloned.1.call-update) | async-done | bytes 1048592 | tf_op jit(solution)/shard_map/reduce_scatter | solution.py:28
  24.9 0.0 copy-done.1
  24.9 1.4 convert_reduce_fusion
  26.3 0.3 fusion.8
  26.6 0.0 copy-done.2
  26.6 0.2 fusion.10
  26.9 2.5 gather_fusion
  29.3 0.2 broadcast_select_fusion
  29.5 0.3 pad_maximum_fusion
  29.8 78.7 %all_to_all.10 = bf16[32,24,2048]{2,1,0:T(8,128)(2,1)} all-to-all(bf16[32,24,2048]{2,1,0:T(8,128)(2,1)S(1)} %pad_maximum_fusion), channel_id=1, replica_groups=mesh['tp'=2,'ep'=16] {'tp','ep'}, dimensions={0} | all-to-all | bytes 6291456 | tf_op jit(solution)/shard_map/all_to_all | solution.py:63
  108.5 22.5 %fusion = f32[32,24,2048]{2,1,0:T(8,128)} fusion(bf16[1,2048,2048]{2,1,0:T(8,128)(2,1)} %param.17, bf16[32,24,2048]{2,1,0:T(8,128)(2,1)} %all_to_all.10, bf16[1,2048,2048]{2,1,0:T(8,128)(2,1)} %param.16), kind=kOutput, calls=%fused_computation.2 | convolution fusion | flops 12888047616 | bytes 26214400 | tf_op jit(solution)/shard_map/smf,fd->smd/dot_general | solution.py:11
  130.9 0.0 copy-start.5
  130.9 4.0 %all-to-all-start.1 = ((f32[32,24,2048]{2,1,0:T(8,128)}), f32[32,24,2048]{2,1,0:T(8,128)}, u32[]{:S(2)}, u32[]{:S(2)}) async-start(f32[32,24,2048]{2,1,0:T(8,128)} %fusion), calls=%async_computation.2 | async-start | bytes 12582912 | tf_op jit(solution)/shard_map/all_to_all | solution.py:67
  134.9 0.0 copy-done.5
  134.9 0.1 copy.25
  135.1 0.1 gt.46
  135.2 0.1 copy.26
  135.4 0.1 mul.85
  135.5 0.1 copy.19
  135.6 141.5 %all-to-all-done.1 = f32[32,24,2048]{2,1,0:T(8,128)} async-done(((f32[32,24,2048]{2,1,0:T(8,128)}), f32[32,24,2048]{2,1,0:T(8,128)}, u32[]{:S(2)}, u32[]{:S(2)}) %all-to-all-start.1) | async-done | bytes 6291488 | tf_op jit(solution)/shard_map/all_to_all | solution.py:67
  277.1 3.6 %reduce_sum.73 = bf16[16,24,2048]{2,1,0:T(8,128)(2,1)S(1)} reduce(f32[2,16,24,2048]{3,2,1,0:T(8,128)} %bitcast.9, f32[]{:T(128)} %constant.17.clone.1), dimensions={0}, to_apply=%region_8.9 | reduce | flops 786432 | bytes 7864324 | tf_op jit(solution)/shard_map/reduce_sum | solution.py:70
  280.7 2.3 gather_fusion.1
  283.1 2.4 reshape.192
  285.5 3.2 %multiply_reduce_fusion = f32[128,2048]{1,0:T(8,128)S(1)} fusion(f32[128,2,2048]{2,1,0:T(2,128)S(1)} %reshape.192, f32[128,2]{1,0:T(8,128)S(1)} %copy.19), kind=kLoop, calls=%fused_computation.8 | loop fusion | flops 786432 | bytes 3146752 | tf_op jit(solution)/shard_map/reduce_sum | solution.py:76
  288.6 0.9 fusion.15
  (13 shorter events, 0.1 us)
Async XLA Ops:
  6.5 1.0 copy-start
  6.5 5.9 %copy-start.3 = (s32[1,128,2]{1,2,0:T(2,128)S(1)}, s32[1,128,2]{1,2,0:T(2,128)}, u32[]{:S(2)}) copy-start(s32[1,128,2]{1,2,0:T(2,128)} %param.15) | copy-start | bytes 3076
  6.5 6.3 %copy-start.4 = (s32[1,128,2]{1,2,0:T(2,128)S(1)}, s32[1,128,2]{1,2,0:T(2,128)}, u32[]{:S(2)}) copy-start(s32[1,128,2]{1,2,0:T(2,128)} %param.13) | copy-start | bytes 3076
  6.5 18.3 %copy-start.1 = (bf16[1,128,2048]{2,1,0:T(8,128)(2,1)S(1)}, bf16[1,128,2048]{2,1,0:T(8,128)(2,1)}, u32[]{:S(2)}) copy-start(bf16[1,128,2048]{2,1,0:T(8,128)(2,1)} %param.11) | copy-start | bytes 1572868
  6.5 18.3 %reduce-scatter.2.cloned.1.call-start = ((), (), s32[]{:S(2)}) async-start(), calls=%async_computation.3 | async-start | bytes 3145728 | tf_op jit(solution)/shard_map/reduce_scatter | solution.py:28
  12.4 14.2 %copy-start.2 = (f32[2048]{0:T(1024)S(1)}, f32[2048]{0:T(1024)}, u32[]{:S(2)}) copy-start(f32[2048]{0:T(1024)} %param.12) | copy-start | bytes 24580
  130.9 4.0 %copy-start.5 = (f32[1,128,2]{1,2,0:T(2,128)S(1)}, f32[1,128,2]{1,2,0:T(2,128)}, u32[]{:S(2)}) copy-start(f32[1,128,2]{1,2,0:T(2,128)} %param.14) | copy-start | bytes 3076
  130.9 146.2 %all-to-all-start.1 = ((f32[32,24,2048]{2,1,0:T(8,128)}), f32[32,24,2048]{2,1,0:T(8,128)}, u32[]{:S(2)}, u32[]{:S(2)}) async-start(f32[32,24,2048]{2,1,0:T(8,128)} %fusion), calls=%async_computation.2 | async-start | bytes 12582912 | tf_op jit(solution)/shard_map/all_to_all | solution.py:67
Sparse Core Ops, SparseCore 0:
  12.5 12.2 reduce-scatter.1
where the time goes:
time: 297 us; the launch traced here: 296 us
  waiting for transfers between devices  152 us (51%)
  blocking collectives  78.7 us (26%)
  matrix products  27.2 us (9%)
  between operations  13.6 us (5%)
  other arithmetic  11.1 us (4%)
  local copies, waits for them, and re-layouts  9.9 us (3%)
  starting transfers between devices  4 us (1%)
    all_to_all x1, waiting for transfers between devices, body(): lax.all_to_all(partial_value, ('tp', 'ep'), split_axis=0, concat_axis=0,...  141 us
    all_to_all x1, blocking collectives, body(): lax.all_to_all(doubled, ('tp', 'ep'), split_axis=0, concat_axis=0, tiled=...  78.7 us
    dot_general x1, matrix products, expert_ffn(): jnp.einsum('smf,fd->smd', hidden, weight_out, preferred_element_type=jnp....  22.5 us
    reduce_scatter x1, waiting for transfers between devices, body(): lax.psum_scatter(jnp.dot(local_context, out_weight, preferred_element_typ...  10.3 us
  transfers between devices with their start and end apart: 2, of which 2 were waited for; matrix products, arithmetic and copies ran while one was open for 1% of the time, Pallas kernels for 0%

commit v1 on v0

v1 whole, which is shorter than its diff:
```python
import functools

import jax
import jax.numpy as jnp
from jax import lax
from jax.experimental import pallas as pl
from jax.experimental.pallas import tpu as pltpu
from jax.sharding import PartitionSpec as P

GROUP = 4
F32 = jnp.float32
BF16 = jnp.bfloat16
MESH = pl.DeviceIdType.MESH


def far_first(step, count):
    odd = step % 2
    return count // 2 + (step // 2) * (1 - odd) - ((step + 1) // 2) * odd


def near_then_far(step, count):
    later = jnp.minimum(step, 1)
    return far_first(jnp.maximum(step - 1, 0), count) * later


def kernel(
    n, cap, cap2,
    ctx, res, gain, raw, wo, w1, w2,
    out,
    wo_v, w1_v, w2_v,
    psend, precv, pown, stream_v, nfull, nrm, meta,
    xsend, xrecv, h_v, yo, ps, pr, ysend, yrecv, mixed, mrecv,
    wsem, pair_send, pair_recv,
    xs_send, xs_recv, fw_send, fw_recv, pt_send, pt_recv, ys_send, ys_recv, self_sem,
):
    tok, width = res.shape
    half = width // 2
    ff = w1.shape[1]
    groups = n // GROUP
    rows = GROUP * cap2
    c = lax.axis_index("tp")
    me = lax.axis_index("ep")
    o = 1 - c
    plane = me // GROUP

    def remote(src, dst, send, recv, **target):
        return pltpu.make_async_remote_copy(
            src_ref=src, dst_ref=dst, send_sem=send, recv_sem=recv,
            device_id=target, device_id_type=MESH,
        )

    load_wo = pltpu.make_async_copy(wo, wo_v, wsem.at[0])
    load_w1 = pltpu.make_async_copy(w1, w1_v, wsem.at[1])
    load_w2 = pltpu.make_async_copy(w2, w2_v, wsem.at[2])
    load_wo.start()
    load_w1.start()
    load_w2.start()

    barrier = pltpu.get_barrier_semaphore()
    pl.semaphore_signal(barrier, inc=1, device_id={"tp": o}, device_id_type=MESH)

    @pl.loop(0, n - 1)
    def _(i):
        pl.semaphore_signal(
            barrier, inc=1, device_id={"ep": (me + 1 + i) % n}, device_id_type=MESH
        )

    experts = lax.broadcasted_iota(jnp.int32, (n, tok), 0).astype(F32)
    before = (
        lax.broadcasted_iota(jnp.int32, (tok, tok), 0)
        < lax.broadcasted_iota(jnp.int32, (tok, tok), 1)
    ).astype(F32).astype(BF16)
    table = raw[...]
    ahead = jnp.zeros((n, 1), F32)
    slots, gates = [], []
    for k in range(2):
        keep = table[2 + k:3 + k]
        hot = jnp.where(experts == table[k:k + 1], keep, 0.0)
        rank = jnp.dot(hot.astype(BF16), before, preferred_element_type=F32) + ahead
        place = jnp.sum(hot * (rank + experts * cap2), axis=0, keepdims=True)
        slots.append(jnp.where(keep > 0, place + (c * cap).astype(F32), -1.0))
        gates.append(jnp.where(keep > 0, table[4 + k:5 + k], 0.0))
        ahead = jnp.sum(hot, axis=1, keepdims=True)
    meta[c] = jnp.concatenate(slots + gates + [jnp.zeros((4, tok), F32)], axis=0)

    load_wo.wait()
    tile = 512

    @pl.loop(0, width // tile)
    def _(t):
        cols = pl.ds(pl.multiple_of(t * tile, tile), tile)
        psend[:, cols] = jnp.dot(
            ctx[pl.ds(o * tok, tok), :], wo_v[:, cols], preferred_element_type=F32
        )

    pl.semaphore_wait(barrier, n)
    send_p = remote(psend, precv, pair_send.at[0], pair_recv.at[0], tp=o)
    send_p.start()
    send_meta = remote(meta.at[c], meta.at[c], pair_send.at[1], pair_recv.at[1], tp=o)
    send_meta.start()

    @pl.loop(0, width // tile)
    def _(t):
        cols = pl.ds(pl.multiple_of(t * tile, tile), tile)
        pown[:, cols] = jnp.dot(
            ctx[pl.ds(c * tok, tok), :], wo_v[:, cols], preferred_element_type=F32
        )

    send_p.wait_recv()

    @pl.loop(0, tok // 16)
    def _(i):
        r = pl.ds(pl.multiple_of(i * 16, 16), 16)
        stream = (res[r, :].astype(F32) + (pown[r, :] + precv[r, :])).astype(BF16)
        stream_v[r, :] = stream
        stream = stream.astype(F32)
        centred = stream - jnp.mean(stream, axis=1, keepdims=True)
        variance = jnp.mean(centred * centred, axis=1, keepdims=True)
        normed = (centred / jnp.sqrt(variance + 1e-05) * gain[...]).astype(BF16)
        nfull[0, r, :] = normed[:, :half]
        nfull[1, r, :] = normed[:, half:]

    send_n = remote(nfull.at[o], nrm.at[c], pair_send.at[2], pair_recv.at[2], tp=o)
    send_n.start()
    nrm[c] = nfull[c]
    remote(meta.at[c], meta.at[o], pair_send.at[1], pair_recv.at[1], tp=o).wait_recv()
    remote(nfull.at[o], nrm.at[o], pair_send.at[2], pair_recv.at[2], tp=o).wait_recv()

    def lanes(row):
        return jnp.concatenate([meta[0, row:row + 1, :], meta[1, row:row + 1, :]], axis=1)

    def matches(q):
        index = (lax.broadcasted_iota(jnp.int32, (rows, 2 * tok), 0) + q * rows).astype(F32)
        return index == lanes(0), index == lanes(1)

    @pl.loop(0, groups)
    def _(step):
        q = (plane + far_first(step, groups)) % groups
        first, second = matches(q)
        pick = jnp.where(first | second, 1.0, 0.0).astype(BF16)
        picked = jnp.dot(
            pick, nrm[...].reshape(2 * tok, half), preferred_element_type=F32
        ).astype(BF16)
        xsend[pl.ds(q * GROUP, GROUP)] = picked.reshape(GROUP, cap2, half)
        for j in range(GROUP):
            e = q * GROUP + j

            @pl.when(e != me)
            def _():
                remote(
                    xsend.at[e], xrecv.at[c, me], xs_send.at[e], xs_recv.at[me], ep=e
                ).start()

            @pl.when(e == me)
            def _():
                pltpu.make_async_copy(xsend.at[e], xrecv.at[c, me], self_sem.at[0]).start()

    load_w1.wait()
    load_w2.wait()

    @pl.loop(0, groups)
    def _(step):
        q = (plane + groups - near_then_far(step, groups)) % groups
        block = pl.ds(q * GROUP, GROUP)
        for j in range(GROUP):
            e = q * GROUP + j

            @pl.when(e != me)
            def _():
                remote(
                    xsend.at[e], xrecv.at[c, e], xs_send.at[e], xs_recv.at[e], ep=e
                ).wait_recv()

            @pl.when(e == me)
            def _():
                pltpu.make_async_copy(xsend.at[e], xrecv.at[c, me], self_sem.at[0]).wait()

        remote(
            xrecv.at[c, block], xrecv.at[c, block], fw_send.at[q], fw_recv.at[q], tp=o
        ).start()
        remote(
            xrecv.at[c, block], xrecv.at[o, block], fw_send.at[q], fw_recv.at[q], tp=o
        ).wait_recv()

        @pl.loop(0, ff // tile)
        def _(t):
            cols = pl.ds(pl.multiple_of(t * tile, tile), tile)
            hidden = jnp.dot(
                xrecv[0, block].reshape(rows, half), w1_v[:half, cols],
                preferred_element_type=F32,
            ) + jnp.dot(
                xrecv[1, block].reshape(rows, half), w1_v[half:, cols],
                preferred_element_type=F32,
            )
            h_v[:, cols] = jnp.maximum(hidden, 0.0).astype(BF16)

        @pl.loop(0, half // tile)
        def _(t):
            cols = pl.ds(pl.multiple_of(t * tile, tile), tile)
            ps[q, :, cols] = jnp.dot(
                h_v[...], w2_v[:, pl.ds(pl.multiple_of(o * half + t * tile, tile), tile)],
                preferred_element_type=F32,
            )

        part = remote(ps.at[q], pr.at[q], pt_send.at[q], pt_recv.at[q], tp=o)
        part.start()

        @pl.loop(0, half // tile)
        def _(t):
            cols = pl.ds(pl.multiple_of(t * tile, tile), tile)
            yo[:, cols] = jnp.dot(
                h_v[...], w2_v[:, pl.ds(pl.multiple_of(c * half + t * tile, tile), tile)],
                preferred_element_type=F32,
            )

        part.wait_recv()
        ysend[block] = (yo[...] + pr[q]).astype(BF16).reshape(GROUP, cap2, half)
        for j in range(GROUP):
            e = q * GROUP + j

            @pl.when(e != me)
            def _():
                remote(
                    ysend.at[e], yrecv.at[me], ys_send.at[e], ys_recv.at[me], ep=e
                ).start()

            @pl.when(e == me)
            def _():
                pltpu.make_async_copy(ysend.at[e], yrecv.at[me], self_sem.at[1]).start()

    mixed[...] = jnp.zeros_like(mixed)

    @pl.loop(0, groups)
    def _(step):
        q = (plane + near_then_far(step, groups)) % groups
        for j in range(GROUP):
            e = q * GROUP + j

            @pl.when(e != me)
            def _():
                remote(
                    ysend.at[e], yrecv.at[e], ys_send.at[e], ys_recv.at[e], ep=e
                ).wait_recv()

            @pl.when(e == me)
            def _():
                pltpu.make_async_copy(ysend.at[e], yrecv.at[me], self_sem.at[1]).wait()

        first, second = matches(q)
        weight = jnp.where(first, lanes(2), 0.0) + jnp.where(second, lanes(3), 0.0)
        high = weight.astype(BF16)
        low = (weight - high.astype(F32)).astype(BF16)
        values = yrecv[pl.ds(q * GROUP, GROUP)].reshape(rows, half)
        dims = (((0,), (0,)), ((), ()))
        added = lax.dot_general(high, values, dims, preferred_element_type=F32)
        added += lax.dot_general(low, values, dims, preferred_element_type=F32)
        mixed[...] += added.reshape(2, tok, half)

    send_m = remote(mixed.at[o], mrecv, pair_send.at[3], pair_recv.at[3], tp=o)
    send_m.start()
    own = pl.ds(pl.multiple_of(c * half, half), half)
    other = pl.ds(pl.multiple_of(o * half, half), half)
    out[:, own] = (stream_v[:, own].astype(F32) + mixed[c]).astype(BF16)
    send_m.wait_recv()
    out[:, other] = (stream_v[:, other].astype(F32) + mrecv[...]).astype(BF16)

    send_p.wait_send()
    send_meta.wait_send()
    send_n.wait_send()
    send_m.wait_send()

    @pl.loop(0, n - 1)
    def _(i):
        e = (me + 1 + i) % n
        remote(xsend.at[e], xrecv.at[c, me], xs_send.at[e], xs_recv.at[me], ep=e).wait_send()
        remote(ysend.at[e], yrecv.at[me], ys_send.at[e], ys_recv.at[me], ep=e).wait_send()

    @pl.loop(0, groups)
    def _(q):
        block = pl.ds(q * GROUP, GROUP)
        remote(
            xrecv.at[c, block], xrecv.at[c, block], fw_send.at[q], fw_recv.at[q], tp=o
        ).wait_send()
        remote(ps.at[q], pr.at[q], pt_send.at[q], pt_recv.at[q], tp=o).wait_send()


def body(
    n,
    context,
    out_weight,
    residual_in,
    norm_gain,
    expert_ids,
    gate_weights,
    keep_mask,
    expert_in,
    expert_out,
):
    tok, width = residual_in.shape[1:]
    heads = out_weight.shape[0]
    ff = expert_in.shape[2]
    half = width // 2
    cap = 3 * tok // n
    cap2 = -(-2 * cap // 16) * 16
    groups = n // GROUP
    rows = GROUP * cap2
    raw = jnp.concatenate(
        [
            expert_ids[0].astype(F32),
            keep_mask[0].astype(F32),
            gate_weights[0],
            jnp.zeros((tok, 2), F32),
        ],
        axis=1,
    ).T
    vmem = pl.BlockSpec(memory_space=pltpu.VMEM)
    hbm = pl.BlockSpec(memory_space=pl.ANY)
    dma = pltpu.SemaphoreType.DMA
    result = pl.pallas_call(
        functools.partial(kernel, n, cap, cap2),
        out_shape=jax.ShapeDtypeStruct((tok, width), BF16),
        in_specs=[vmem, vmem, vmem, vmem, hbm, hbm, hbm],
        out_specs=vmem,
        scratch_shapes=[
            pltpu.VMEM((heads, width), BF16),
            pltpu.VMEM((width, ff), BF16),
            pltpu.VMEM((ff, width), BF16),
            pltpu.VMEM((tok, width), F32),
            pltpu.VMEM((tok, width), F32),
            pltpu.VMEM((tok, width), F32),
            pltpu.VMEM((tok, width), BF16),
            pltpu.VMEM((2, tok, half), BF16),
            pltpu.VMEM((2, tok, half), BF16),
            pltpu.VMEM((2, 8, tok), F32),
            pltpu.VMEM((n, cap2, half), BF16),
            pltpu.VMEM((2, n, cap2, half), BF16),
            pltpu.VMEM((rows, ff), BF16),
            pltpu.VMEM((rows, half), F32),
            pltpu.VMEM((groups, rows, half), F32),
            pltpu.VMEM((groups, rows, half), F32),
            pltpu.VMEM((n, cap2, half), BF16),
            pltpu.VMEM((n, cap2, half), BF16),
            pltpu.VMEM((2, tok, half), F32),
            pltpu.VMEM((tok, half), F32),
            dma((3,)), dma((4,)), dma((4,)),
            dma((n,)), dma((n,)), dma((groups,)), dma((groups,)),
            dma((groups,)), dma((groups,)), dma((n,)), dma((n,)), dma((2,)),
        ],
        compiler_params=pltpu.CompilerParams(
            collective_id=0, has_side_effects=True, vmem_limit_bytes=60 * 2**20
        ),
    )(context[0], residual_in[0], norm_gain[None, :], raw, out_weight, expert_in[0], expert_out[0])
    return result[None]


def solution(mesh):
    return jax.shard_map(
        functools.partial(body, mesh.shape["ep"]),
        mesh=mesh,
        in_specs=(
            P("ep", None, "tp"),
            P("tp", None),
            P("ep", "tp", None),
            P(),
            P("ep", "tp", None),
            P("ep", "tp", None),
            P("ep", "tp", None),
            P("ep", None, "tp"),
            P("ep", "tp", None),
        ),
        out_specs=P("ep", "tp", None),
        check_vma=False,
    )
```

time: 297 us -> 96.1 us (0.32)
  the two profiles are of different devices: /device:TPU:0 before, /device:TPU:31 now
where the time goes in v1:
time: 96.1 us; the launch traced here: 95.9 us
  Pallas kernels  91.9 us (96%)
  other arithmetic  2.04 us (2%)
  local copies, waits for them, and re-layouts  1.96 us (2%)
    pallas_call x1, Pallas kernels, body(): pl.pallas_call(functools.partial(kernel, n, cap, cap2), out_shape=jax.Sha...  91.9 us

profile of v1, /device:TPU:31, one launch (start us, length us, event | category | flops | bytes accessed | tf_op | source)
XLA Modules:
  0.0 95.9 jit_solution(910527779105957365)
XLA Ops:
  0.0 0.1 pad.3.clone
  0.1 0.7 convert_bitcast_fusion
  0.8 1.3 %maximum_bitcast_fusion.raw = f32[8,128]{1,0:T(8,128)} fusion(f32[128,2]{0,1:T(2,128)} %bitcast.19, f32[128,2]{0,1:T(2,128)S(1)} %get-tuple-element.5, f32[128,2]{0,1:T(2,128)S(1)} %get-tuple-element.6, f32[8]{0:T(128)S(1)} %pad.3.clone), kind=kLoop, calls=%fused_computation | loop fusion | flops 3072 | bytes 7200 | tf_op jit(solution)/shard_map/transpose | solution.py:315
  2.1 91.9 %shard_map.91 = bf16[128,2048]{1,0:T(8,128)(2,1)} custom-call(bf16[256,1024]{1,0:T(8,128)(2,1)} %bitcast.16, bf16[128,2048]{1,0:T(8,128)(2,1)} %bitcast.17, f32[1,2048]{1,0:T(1,128)} %bitcast.18, f32[8,128]{1,0:T(8,128)} %maximum_bitcast_fusion.raw, bf16[1024,2048]{1,0:T(8,128)(2,1)} %wo.1, bf16[2048,2048]{1,0:T(8,128)(2,1)} %bitcast.13, ...), custom_call_target="tpu_custom_call" | custom-call | tf_op jit(solution)/shard_map/pallas_call | solution.py:319
  94.0 1.9 %copy.11 = bf16[1,128,2048]{2,1,0:T(8,128)(2,1)} copy(bf16[1,128,2048]{2,1,0:T(8,128)(2,1)} %bitcast.15) | data formatting | bytes 1048576
  (1 shorter events, 0.0 us)

commit v2 on v1

--- a/solution.py
+++ b/solution.py
@@ -25,10 +25,10 @@
 
 def kernel(
     n, cap, cap2,
-    ctx, res, gain, raw, wo, w1, w2,
+    ctx, res, gain, ids, gate, kept, wo, w1, w2,
     out,
     wo_v, w1_v, w2_v,
-    psend, precv, pown, stream_v, nfull, nrm, meta,
+    both, precv, stream_v, nfull, nrm, meta,
     xsend, xrecv, h_v, yo, ps, pr, ysend, yrecv, mixed, mrecv,
     wsem, pair_send, pair_recv,
     xs_send, xs_recv, fw_send, fw_recv, pt_send, pt_recv, ys_send, ys_recv, self_sem,
@@ -49,12 +49,18 @@
             device_id=target, device_id_type=MESH,
         )
 
-    load_wo = pltpu.make_async_copy(wo, wo_v, wsem.at[0])
-    load_w1 = pltpu.make_async_copy(w1, w1_v, wsem.at[1])
-    load_w2 = pltpu.make_async_copy(w2, w2_v, wsem.at[2])
-    load_wo.start()
-    load_w1.start()
-    load_w2.start()
+    tile = 512
+    tiles = width // tile
+    load_wo = [
+        pltpu.make_async_copy(
+            wo.at[:, t * tile:(t + 1) * tile], wo_v.at[:, t * tile:(t + 1) * tile], wsem.at[2 + t]
+        )
+        for t in range(tiles)
+    ]
+    load_w1 = pltpu.make_async_copy(w1, w1_v, wsem.at[0])
+    load_w2 = pltpu.make_async_copy(w2, w2_v, wsem.at[1])
+    for load in load_wo:
+        load.start()
 
     barrier = pltpu.get_barrier_semaphore()
     pl.semaphore_signal(barrier, inc=1, device_id={"tp": o}, device_id_type=MESH)
@@ -70,61 +76,71 @@
         lax.broadcasted_iota(jnp.int32, (tok, tok), 0)
         < lax.broadcasted_iota(jnp.int32, (tok, tok), 1)
     ).astype(F32).astype(BF16)
-    table = raw[...]
     ahead = jnp.zeros((n, 1), F32)
     slots, gates = [], []
     for k in range(2):
-        keep = table[2 + k:3 + k]
-        hot = jnp.where(experts == table[k:k + 1], keep, 0.0)
+        keep = kept[k:k + 1].astype(F32)
+        hot = jnp.where(experts == ids[k:k + 1].astype(F32), keep, 0.0)
         rank = jnp.dot(hot.astype(BF16), before, preferred_element_type=F32) + ahead
         place = jnp.sum(hot * (rank + experts * cap2), axis=0, keepdims=True)
         slots.append(jnp.where(keep > 0, place + (c * cap).astype(F32), -1.0))
-        gates.append(jnp.where(keep > 0, table[4 + k:5 + k], 0.0))
+        gates.append(jnp.where(keep > 0, gate[k:k + 1], 0.0))
         ahead = jnp.sum(hot, axis=1, keepdims=True)
     meta[c] = jnp.concatenate(slots + gates + [jnp.zeros((4, tok), F32)], axis=0)
 
-    load_wo.wait()
-    tile = 512
-
-    @pl.loop(0, width // tile)
-    def _(t):
-        cols = pl.ds(pl.multiple_of(t * tile, tile), tile)
-        psend[:, cols] = jnp.dot(
-            ctx[pl.ds(o * tok, tok), :], wo_v[:, cols], preferred_element_type=F32
-        )
-
-    pl.semaphore_wait(barrier, n)
-    send_p = remote(psend, precv, pair_send.at[0], pair_recv.at[0], tp=o)
-    send_p.start()
+    send_p = []
+    for t in range(tiles):
+        cols = pl.ds(t * tile, tile)
+        load_wo[t].wait()
+        if t == tiles - 1:
+            load_w1.start()
+            load_w2.start()
+        both[:, :, cols] = jnp.dot(
+            ctx[...], wo_v[:, cols], preferred_element_type=F32
+        ).reshape(2, tok, tile)
+        if t == 0:
+            pl.semaphore_wait(barrier, n)
+        send_p.append(remote(
+            both.at[o, :, cols], precv.at[:, cols],
+            pair_send.at[4 + t], pair_recv.at[4 + t], tp=o,
+        ))
+        send_p[t].start()
     send_meta = remote(meta.at[c], meta.at[c], pair_send.at[1], pair_recv.at[1], tp=o)
     send_meta.start()
-
-    @pl.loop(0, width // tile)
-    def _(t):
-        cols = pl.ds(pl.multiple_of(t * tile, tile), tile)
-        pown[:, cols] = jnp.dot(
-            ctx[pl.ds(c * tok, tok), :], wo_v[:, cols], preferred_element_type=F32
-        )
-
-    send_p.wait_recv()
-
-    @pl.loop(0, tok // 16)
-    def _(i):
-        r = pl.ds(pl.multiple_of(i * 16, 16), 16)
-        stream = (res[r, :].astype(F32) + (pown[r, :] + precv[r, :])).astype(BF16)
-        stream_v[r, :] = stream
-        stream = stream.astype(F32)
-        centred = stream - jnp.mean(stream, axis=1, keepdims=True)
-        variance = jnp.mean(centred * centred, axis=1, keepdims=True)
-        normed = (centred / jnp.sqrt(variance + 1e-05) * gain[...]).astype(BF16)
-        nfull[0, r, :] = normed[:, :half]
-        nfull[1, r, :] = normed[:, half:]
-
-    send_n = remote(nfull.at[o], nrm.at[c], pair_send.at[2], pair_recv.at[2], tp=o)
-    send_n.start()
-    nrm[c] = nfull[c]
+    for send in send_p:
+        send.wait_recv()
+
+    send_n = []
+    for part in range(2):
+        top = part * (tok // 2)
+
+        @pl.loop(0, tok // 32, unroll=2)
+        def _(i):
+            r = pl.ds(pl.multiple_of(top + i * 16, 16), 16)
+            stream = (res[r, :].astype(F32) + (both[c, r, :] + precv[r, :])).astype(BF16)
+            stream_v[r, :] = stream
+            stream = stream.astype(F32)
+            centred = stream - jnp.mean(stream, axis=1, keepdims=True)
+            variance = jnp.mean(centred * centred, axis=1, keepdims=True)
+            normed = (centred * (1.0 / jnp.sqrt(variance + 1e-05)) * gain[...]).astype(BF16)
+            nfull[0, r, :] = normed[:, :half]
+            nfull[1, r, :] = normed[:, half:]
+
+        r = pl.ds(top, tok // 2)
+        sem = 2 * part
+        send_n.append(remote(
+            nfull.at[o, r], nrm.at[c, r], pair_send.at[sem], pair_recv.at[sem], tp=o
+        ))
+        send_n[part].start()
+        nrm[c, r] = nfull[c, r]
+
     remote(meta.at[c], meta.at[o], pair_send.at[1], pair_recv.at[1], tp=o).wait_recv()
-    remote(nfull.at[o], nrm.at[o], pair_send.at[2], pair_recv.at[2], tp=o).wait_recv()
+    for part in range(2):
+        r = pl.ds(part * (tok // 2), tok // 2)
+        sem = 2 * part
+        remote(
+            nfull.at[o, r], nrm.at[o, r], pair_send.at[sem], pair_recv.at[sem], tp=o
+        ).wait_recv()
 
     def lanes(row):
         return jnp.concatenate([meta[0, row:row + 1, :], meta[1, row:row + 1, :]], axis=1)
@@ -264,9 +280,9 @@
     send_m.wait_recv()
     out[:, other] = (stream_v[:, other].astype(F32) + mrecv[...]).astype(BF16)
 
-    send_p.wait_send()
+    for send in send_p + send_n:
+        send.wait_send()
     send_meta.wait_send()
-    send_n.wait_send()
     send_m.wait_send()
 
     @pl.loop(0, n - 1)
@@ -304,29 +320,19 @@
     cap2 = -(-2 * cap // 16) * 16
     groups = n // GROUP
     rows = GROUP * cap2
-    raw = jnp.concatenate(
-        [
-            expert_ids[0].astype(F32),
-            keep_mask[0].astype(F32),
-            gate_weights[0],
-            jnp.zeros((tok, 2), F32),
-        ],
-        axis=1,
-    ).T
     vmem = pl.BlockSpec(memory_space=pltpu.VMEM)
     hbm = pl.BlockSpec(memory_space=pl.ANY)
     dma = pltpu.SemaphoreType.DMA
     result = pl.pallas_call(
         functools.partial(kernel, n, cap, cap2),
         out_shape=jax.ShapeDtypeStruct((tok, width), BF16),
-        in_specs=[vmem, vmem, vmem, vmem, hbm, hbm, hbm],
+        in_specs=[vmem] * 6 + [hbm, hbm, hbm],
         out_specs=vmem,
         scratch_shapes=[
             pltpu.VMEM((heads, width), BF16),
             pltpu.VMEM((width, ff), BF16),
             pltpu.VMEM((ff, width), BF16),
-            pltpu.VMEM((tok, width), F32),
-            pltpu.VMEM((tok, width), F32),
+            pltpu.VMEM((2, tok, width), F32),
             pltpu.VMEM((tok, width), F32),
             pltpu.VMEM((tok, width), BF16),
             pltpu.VMEM((2, tok, half), BF16),
@@ -342,14 +348,18 @@
             pltpu.VMEM((n, cap2, half), BF16),
             pltpu.VMEM((2, tok, half), F32),
             pltpu.VMEM((tok, half), F32),
-            dma((3,)), dma((4,)), dma((4,)),
+            dma((6,)), dma((8,)), dma((8,)),
             dma((n,)), dma((n,)), dma((groups,)), dma((groups,)),
             dma((groups,)), dma((groups,)), dma((n,)), dma((n,)), dma((2,)),
         ],
         compiler_params=pltpu.CompilerParams(
             collective_id=0, has_side_effects=True, vmem_limit_bytes=60 * 2**20
         ),
-    )(context[0], residual_in[0], norm_gain[None, :], raw, out_weight, expert_in[0], expert_out[0])
+    )(
+        context[0], residual_in[0], norm_gain[None, :],
+        expert_ids[0].T, gate_weights[0].T, keep_mask[0].T,
+        out_weight, expert_in[0], expert_out[0],
+    )
     return result[None]
 
 

time: 96.1 us -> 93.3 us (0.971)
  other arithmetic: 2.04 us -> 0 us
    transpose x1 -> x0, other arithmetic: 1.34 us -> none  [body(): raw = jnp.concatenate([expert_ids[0].astype(F32), keep_mask[0].astype(F32...]
where the time goes in v2:
time: 93.3 us; the launch traced here: 93.1 us
  Pallas kernels  91.2 us (98%)
  local copies, waits for them, and re-layouts  1.88 us (2%)
    pallas_call x1, Pallas kernels, body(): pl.pallas_call(functools.partial(kernel, n, cap, cap2), out_shape=jax.Sha...  91.2 us
    unnamed x1, local copies, waits for them, and re-layouts  1.88 us

profile of v2, /device:TPU:31, one launch (start us, length us, event | category | flops | bytes accessed | tf_op | source)
XLA Modules:
  0.0 93.1 jit_solution(8437871923827872186)
XLA Ops:
  0.0 91.2 %shard_map.91 = bf16[128,2048]{1,0:T(8,128)(2,1)} custom-call(bf16[256,1024]{1,0:T(8,128)(2,1)} %bitcast.18, bf16[128,2048]{1,0:T(8,128)(2,1)} %bitcast.19, f32[1,2048]{1,0:T(1,128)} %bitcast.20, s32[2,128]{1,0:T(2,128)} %bitcast.21, f32[2,128]{1,0:T(2,128)} %bitcast.22, s32[2,128]{1,0:T(2,128)} %bitcast.23, bf16[1024,2048]{1,0:T(8,128)(2,1)} %wo.1, ...), custom_call_target="tpu_custom_call" | custom-call | tf_op jit(solution)/shard_map/pallas_call | solution.py:326
  91.2 1.9 %copy.11 = bf16[1,128,2048]{2,1,0:T(8,128)(2,1)} copy(bf16[1,128,2048]{2,1,0:T(8,128)(2,1)} %bitcast.17) | data formatting | bytes 1048576

commit v3 on v2

v3 whole, which is shorter than its diff:
```python
import functools

import jax
import jax.numpy as jnp
from jax import lax
from jax.experimental import pallas as pl
from jax.experimental.pallas import tpu as pltpu
from jax.sharding import PartitionSpec as P

F32 = jnp.float32
BF16 = jnp.bfloat16
MESH = pl.DeviceIdType.MESH


def kernel(
    n, cap, cap2, caps,
    ctx, res, gain, ids, gate, kept, wo, w1, w2,
    out,
    wo_v, w1_v, w2_v,
    both, precv, stream_v, nfull, nrm, meta, pnrm, pmeta,
    xsend, xrecv, fsend, frecv, h_v, yo, ps, pr, fpr,
    ysend, yrecv, fysend, fyrecv, cback, cmix, mixed, mrecv,
    wsem, pair_send, pair_recv, tk_send, tk_recv, fw_send, fw_recv, pt_send, pt_recv,
    xs_send, xs_recv, ys_send, ys_recv, ff_send, ff_recv, fy_send, fy_recv,
    cb_send, cb_recv, self_sem,
):
    tok, width = res.shape
    half = width // 2
    ff = w1.shape[1]
    near = n // 2
    c = lax.axis_index("tp")
    me = lax.axis_index("ep")
    o = 1 - c
    base = me // near * near
    mine = me - base
    partner = (me + near) % n

    def remote(src, dst, send, recv, **target):
        return pltpu.make_async_remote_copy(
            src_ref=src, dst_ref=dst, send_sem=send, recv_sem=recv,
            device_id=target, device_id_type=MESH,
        )

    tile = 512
    tiles = width // tile
    load_wo = [
        pltpu.make_async_copy(
            wo.at[:, t * tile:(t + 1) * tile], wo_v.at[:, t * tile:(t + 1) * tile], wsem.at[2 + t]
        )
        for t in range(tiles)
    ]
    load_w1 = pltpu.make_async_copy(w1, w1_v, wsem.at[0])
    load_w2 = pltpu.make_async_copy(w2, w2_v, wsem.at[1])
    for load in load_wo:
        load.start()

    barrier = pltpu.get_barrier_semaphore()
    pl.semaphore_signal(barrier, inc=1, device_id={"tp": o}, device_id_type=MESH)

    pl.semaphore_signal(barrier, inc=1, device_id={"ep": partner}, device_id_type=MESH)

    @pl.loop(0, near - 1)
    def _(i):
        pl.semaphore_signal(
            barrier, inc=1, device_id={"ep": base + (mine + 1 + i) % near}, device_id_type=MESH
        )

    experts = lax.broadcasted_iota(jnp.int32, (n, tok), 0).astype(F32)
    before = (
        lax.broadcasted_iota(jnp.int32, (tok, tok), 0)
        < lax.broadcasted_iota(jnp.int32, (tok, tok), 1)
    ).astype(F32).astype(BF16)
    ahead = jnp.zeros((n, 1), F32)
    slots, gates, places = [], [], []
    for k in range(2):
        keep = kept[k:k + 1].astype(F32)
        hot = jnp.where(experts == ids[k:k + 1].astype(F32), keep, 0.0)
        rank = jnp.dot(hot.astype(BF16), before, preferred_element_type=F32) + ahead
        place = jnp.sum(hot * (rank + experts * cap2), axis=0, keepdims=True)
        slots.append(jnp.where(keep > 0, place + (c * cap).astype(F32), -1.0))
        gates.append(jnp.where(keep > 0, gate[k:k + 1], 0.0))
        place = jnp.sum(hot * (rank + experts * caps), axis=0, keepdims=True)
        places.append(jnp.where(keep > 0, place, -1.0))
        ahead = jnp.sum(hot, axis=1, keepdims=True)
    meta[c] = jnp.concatenate(slots + gates + places + [jnp.zeros((2, tok), F32)], axis=0)

    send_p = []
    for t in range(tiles):
        cols = pl.ds(t * tile, tile)
        load_wo[t].wait()
        if t == tiles - 1:
            load_w1.start()
            load_w2.start()
        both[:, :, cols] = jnp.dot(
            ctx[...], wo_v[:, cols], preferred_element_type=F32
        ).reshape(2, tok, tile)
        if t == 0:
            pl.semaphore_wait(barrier, near + 1)
        send_p.append(remote(
            both.at[o, :, cols], precv.at[:, cols],
            pair_send.at[4 + t], pair_recv.at[4 + t], tp=o,
        ))
        send_p[t].start()
    send_meta = remote(meta.at[c], meta.at[c], pair_send.at[1], pair_recv.at[1], tp=o)
    send_meta.start()
    for send in send_p:
        send.wait_recv()

    send_n = []
    for part in range(2):
        top = part * (tok // 2)

        @pl.loop(0, tok // 32, unroll=2)
        def _(i):
            r = pl.ds(pl.multiple_of(top + i * 16, 16), 16)
            stream = (res[r, :].astype(F32) + (both[c, r, :] + precv[r, :])).astype(BF16)
            stream_v[r, :] = stream
            stream = stream.astype(F32)
            centred = stream - jnp.mean(stream, axis=1, keepdims=True)
            variance = jnp.mean(centred * centred, axis=1, keepdims=True)
            normed = (centred * (1.0 / jnp.sqrt(variance + 1e-05)) * gain[...]).astype(BF16)
            nfull[0, r, :] = normed[:, :half]
            nfull[1, r, :] = normed[:, half:]

        r = pl.ds(top, tok // 2)
        sem = 2 * part
        send_n.append(remote(
            nfull.at[o, r], nrm.at[c, r], pair_send.at[sem], pair_recv.at[sem], tp=o
        ))
        send_n[part].start()
        nrm[c, r] = nfull[c, r]

    remote(meta.at[c], meta.at[o], pair_send.at[1], pair_recv.at[1], tp=o).wait_recv()
    for part in range(2):
        r = pl.ds(part * (tok // 2), tok // 2)
        sem = 2 * part
        remote(
            nfull.at[o, r], nrm.at[o, r], pair_send.at[sem], pair_recv.at[sem], tp=o
        ).wait_recv()

    def lanes(row):
        return jnp.concatenate([meta[0, row:row + 1, :], meta[1, row:row + 1, :]], axis=1)

    def near_matches():
        shape = (near * cap2, 2 * tok)
        index = (lax.broadcasted_iota(jnp.int32, shape, 0) + base * cap2).astype(F32)
        return index == lanes(0), index == lanes(1)

    def far_matches(s):
        shape = (near * caps, tok)
        index = (lax.broadcasted_iota(jnp.int32, shape, 0) + base * caps).astype(F32)
        return index == pmeta[s, 4:5, :], index == pmeta[s, 5:6, :]

    def picked(matches, tokens, shape):
        pick = jnp.where(matches[0] | matches[1], 1.0, 0.0).astype(BF16)
        return jnp.dot(pick, tokens, preferred_element_type=F32).astype(BF16).reshape(shape)

    def spread(src, dst, send, recv, first, own):
        @pl.loop(0, near)
        def _(j):
            @pl.when(j != mine)
            def _():
                remote(
                    src.at[j], dst.at[mine], send.at[first + j], recv.at[first + mine],
                    ep=base + j,
                ).start()

            @pl.when(j == mine)
            def _():
                pltpu.make_async_copy(src.at[j], dst.at[j], self_sem.at[own]).start()

    def gathered(src, dst, send, recv, first, own):
        @pl.loop(0, near)
        def _(j):
            @pl.when(j != mine)
            def _():
                remote(
                    src.at[j], dst.at[j], send.at[first + j], recv.at[first + j], ep=base + j
                ).wait_recv()

            @pl.when(j == mine)
            def _():
                pltpu.make_async_copy(src.at[j], dst.at[j], self_sem.at[own]).wait()

    def drained(src, dst, send, recv, first):
        @pl.loop(0, near)
        def _(j):
            @pl.when(j != mine)
            def _():
                remote(
                    src.at[j], dst.at[j], send.at[first + j], recv.at[first + j], ep=base + j
                ).wait_send()

    def forward(x, k):
        return remote(x.at[c], x.at[c], fw_send.at[k], fw_recv.at[k], tp=o)

    def expert(x, part_recv, y, k):
        rows = x.shape[1] * x.shape[2]
        part_send = ps.at[:rows]
        forward(x, k).start()
        remote(x.at[c], x.at[o], fw_send.at[k], fw_recv.at[k], tp=o).wait_recv()

        @pl.loop(0, ff // tile)
        def _(t):
            cols = pl.ds(pl.multiple_of(t * tile, tile), tile)
            hidden = jnp.dot(
                x[0].reshape(rows, half), w1_v[:half, cols], preferred_element_type=F32
            ) + jnp.dot(
                x[1].reshape(rows, half), w1_v[half:, cols], preferred_element_type=F32
            )
            h_v[:rows, cols] = jnp.maximum(hidden, 0.0).astype(BF16)

        def second(dst, side):
            @pl.loop(0, half // tile)
            def _(t):
                cols = pl.ds(pl.multiple_of(t * tile, tile), tile)
                dst[:, cols] = jnp.dot(
                    h_v[:rows], w2_v[:, pl.ds(pl.multiple_of(side * half + t * tile, tile), tile)],
                    preferred_element_type=F32,
                )

        second(part_send, o)
        part = remote(part_send, part_recv, pt_send.at[k], pt_recv.at[k], tp=o)
        part.start()
        second(yo.at[:rows], c)
        part.wait()
        y[...] = (yo[:rows] + part_recv[...]).astype(BF16).reshape(y.shape)

    def weighted(matches, gate0, gate1, values):
        weight = jnp.where(matches[0], gate0, 0.0) + jnp.where(matches[1], gate1, 0.0)
        high = weight.astype(BF16)
        low = (weight - high.astype(F32)).astype(BF16)
        dims = (((0,), (0,)), ((), ()))
        return lax.dot_general(
            high, values, dims, preferred_element_type=F32
        ) + lax.dot_general(low, values, dims, preferred_element_type=F32)

    def to_partner(s):
        return remote(nrm.at[s], pnrm.at[s], tk_send.at[s], tk_recv.at[s], ep=partner)

    def far_rows(s):
        to_partner(s).wait_recv()
        fsend[s] = picked(far_matches(s), pnrm[s], (near, caps, half))
        spread(fsend.at[s], frecv.at[s, c], ff_send, ff_recv, s * near, 2 + s)

    def far_expert(s):
        gathered(fsend.at[s], frecv.at[s, c], ff_send, ff_recv, s * near, 2 + s)
        expert(frecv.at[s], fpr.at[s], fysend.at[s], 1 + s)
        spread(fysend.at[s], fyrecv.at[s], fy_send, fy_recv, s * near, 4 + s)

    def back(s):
        return remote(cback.at[s], cmix.at[s], cb_send.at[s], cb_recv.at[s], ep=partner)

    def far_back(s):
        gathered(fysend.at[s], fyrecv.at[s], fy_send, fy_recv, s * near, 4 + s)
        cback[s] = weighted(
            far_matches(s), pmeta[s, 2:3, :], pmeta[s, 3:4, :],
            fyrecv[s].reshape(near * caps, half),
        ).astype(BF16)
        back(s).start()

    give_meta = remote(meta, pmeta, tk_send.at[2], tk_recv.at[2], ep=partner)
    give_meta.start()
    to_partner(0).start()
    xsend[...] = picked(near_matches(), nrm[...].reshape(2 * tok, half), (near, cap2, half))
    spread(xsend, xrecv.at[c], xs_send, xs_recv, 0, 0)
    to_partner(0).wait_send()
    to_partner(1).start()
    give_meta.wait_recv()
    far_rows(0)
    load_w1.wait()
    load_w2.wait()
    gathered(xsend, xrecv.at[c], xs_send, xs_recv, 0, 0)
    expert(xrecv, pr, ysend, 0)
    spread(ysend, yrecv, ys_send, ys_recv, 0, 1)
    far_expert(0)
    far_rows(1)
    far_back(0)
    far_expert(1)
    gathered(ysend, yrecv, ys_send, ys_recv, 0, 1)
    mixed[...] = weighted(
        near_matches(), lanes(2), lanes(3), yrecv[...].reshape(near * cap2, half)
    ).reshape(2, tok, half)
    far_back(1)
    for s in range(2):
        back(s).wait_recv()
        mixed[s] += cmix[s].astype(F32)

    send_m = remote(mixed.at[o], mrecv, pair_send.at[3], pair_recv.at[3], tp=o)
    send_m.start()
    own = pl.ds(pl.multiple_of(c * half, half), half)
    other = pl.ds(pl.multiple_of(o * half, half), half)
    out[:, own] = (stream_v[:, own].astype(F32) + mixed[c]).astype(BF16)
    send_m.wait_recv()
    out[:, other] = (stream_v[:, other].astype(F32) + mrecv[...]).astype(BF16)

    for send in send_p + send_n:
        send.wait_send()
    send_meta.wait_send()
    send_m.wait_send()

    give_meta.wait_send()
    to_partner(1).wait_send()
    drained(xsend, xrecv.at[c], xs_send, xs_recv, 0)
    drained(ysend, yrecv, ys_send, ys_recv, 0)
    forward(xrecv, 0).wait_send()
    for s in range(2):
        drained(fsend.at[s], frecv.at[s, c], ff_send, ff_recv, s * near)
        drained(fysend.at[s], fyrecv.at[s], fy_send, fy_recv, s * near)
        forward(frecv.at[s], 1 + s).wait_send()
        back(s).wait_send()


def body(
    n,
    context,
    out_weight,
    residual_in,
    norm_gain,
    expert_ids,
    gate_weights,
    keep_mask,
    expert_in,
    expert_out,
):
    tok, width = residual_in.shape[1:]
    heads = out_weight.shape[0]
    ff = expert_in.shape[2]
    half = width // 2
    cap = 3 * tok // n
    cap2 = -(-2 * cap // 16) * 16
    caps = -(-cap // 16) * 16
    near = n // 2
    wide, narrow = near * cap2, near * caps
    vmem = pl.BlockSpec(memory_space=pltpu.VMEM)
    hbm = pl.BlockSpec(memory_space=pl.ANY)
    dma = pltpu.SemaphoreType.DMA
    result = pl.pallas_call(
        functools.partial(kernel, n, cap, cap2, caps),
        out_shape=jax.ShapeDtypeStruct((tok, width), BF16),
        in_specs=[vmem] * 6 + [hbm, hbm, hbm],
        out_specs=vmem,
        scratch_shapes=[
            pltpu.VMEM((heads, width), BF16),
            pltpu.VMEM((width, ff), BF16),
            pltpu.VMEM((ff, width), BF16),
            pltpu.VMEM((2, tok, width), F32),
            pltpu.VMEM((tok, width), F32),
            pltpu.VMEM((tok, width), BF16),
            pltpu.VMEM((2, tok, half), BF16),
            pltpu.VMEM((2, tok, half), BF16),
            pltpu.VMEM((2, 8, tok), F32),
            pltpu.VMEM((2, tok, half), BF16),
            pltpu.VMEM((2, 8, tok), F32),
            pltpu.VMEM((near, cap2, half), BF16),
            pltpu.VMEM((2, near, cap2, half), BF16),
            pltpu.VMEM((2, near, caps, half), BF16),
            pltpu.VMEM((2, 2, near, caps, half), BF16),
            pltpu.VMEM((max(wide, narrow), ff), BF16),
            pltpu.VMEM((max(wide, narrow), half), F32),
            pltpu.VMEM((max(wide, narrow), half), F32),
            pltpu.VMEM((wide, half), F32),
            pltpu.VMEM((2, narrow, half), F32),
            pltpu.VMEM((near, cap2, half), BF16),
            pltpu.VMEM((near, cap2, half), BF16),
            pltpu.VMEM((2, near, caps, half), BF16),
            pltpu.VMEM((2, near, caps, half), BF16),
            pltpu.VMEM((2, tok, half), BF16),
            pltpu.VMEM((2, tok, half), BF16),
            pltpu.VMEM((2, tok, half), F32),
            pltpu.VMEM((tok, half), F32),
            dma((6,)), dma((8,)), dma((8,)), dma((3,)), dma((3,)),
            dma((3,)), dma((3,)), dma((3,)), dma((3,)),
            dma((near,)), dma((near,)), dma((near,)), dma((near,)),
            dma((n,)), dma((n,)), dma((n,)), dma((n,)),
            dma((2,)), dma((2,)), dma((6,)),
        ],
        compiler_params=pltpu.CompilerParams(
            collective_id=0, has_side_effects=True, vmem_limit_bytes=60 * 2**20
        ),
    )(
        context[0], residual_in[0], norm_gain[None, :],
        expert_ids[0].T, gate_weights[0].T, keep_mask[0].T,
        out_weight, expert_in[0], expert_out[0],
    )
    return result[None]


def solution(mesh):
    return jax.shard_map(
        functools.partial(body, mesh.shape["ep"]),
        mesh=mesh,
        in_specs=(
            P("ep", None, "tp"),
            P("tp", None),
            P("ep", "tp", None),
            P(),
            P("ep", "tp", None),
            P("ep", "tp", None),
            P("ep", "tp", None),
            P("ep", None, "tp"),
            P("ep", "tp", None),
        ),
        out_specs=P("ep", "tp", None),
        check_vma=False,
    )
```

time: 93.3 us -> 100 us (1.072); the launches traced: 93.1 us -> 98.2 us
  Pallas kernels: 91.2 us -> 96.3 us
    pallas_call x1, Pallas kernels: 91.2 us -> 96.3 us  [body(): pl.pallas_call(functools.partial(kernel, n, cap, cap2, caps), out_shape=j...]
where the time goes in v3:
time: 100 us; the launch traced here: 98.2 us
  Pallas kernels  96.3 us (96%)
  local copies, waits for them, and re-layouts  1.88 us (2%)
    pallas_call x1, Pallas kernels, body(): pl.pallas_call(functools.partial(kernel, n, cap, cap2, caps), out_shape=j...  96.3 us

profile of v3, /device:TPU:31, one launch (start us, length us, event | category | flops | bytes accessed | tf_op | source)
XLA Modules:
  0.0 98.2 jit_solution(9477573263604059954)
XLA Ops:
  0.0 96.3 %shard_map.91 = bf16[128,2048]{1,0:T(8,128)(2,1)} custom-call(bf16[256,1024]{1,0:T(8,128)(2,1)} %bitcast.18, bf16[128,2048]{1,0:T(8,128)(2,1)} %bitcast.19, f32[1,2048]{1,0:T(1,128)} %bitcast.20, s32[2,128]{1,0:T(2,128)} %bitcast.21, f32[2,128]{1,0:T(2,128)} %bitcast.22, s32[2,128]{1,0:T(2,128)} %bitcast.23, bf16[1024,2048]{1,0:T(8,128)(2,1)} %wo.1, ...), custom_call_target="tpu_custom_call" | custom-call | tf_op jit(solution)/shard_map/pallas_call | solution.py:338
  96.3 1.9 %copy.11 = bf16[1,128,2048]{2,1,0:T(8,128)(2,1)} copy(bf16[1,128,2048]{2,1,0:T(8,128)(2,1)} %bitcast.17) | data formatting | bytes 1048576
